TPU v7x, 1024 devices: a whole 8x8x8 slice. The times are simulated.
1024 devices in a mesh: row: 32 (over x, y_lo, core), col: 32 (over y_hi, z).
Axes of the slice: x: 8, y: 8 (y_hi: 4, y_lo: 2; y = y_hi * 2 + y_lo), z: 8, core: 2. Of those that a mesh axis runs over, the one named last changes fastest.
Arguments:
- x_block: float32 [8, 262144], P(None, ('row', 'col')), may hold values from -45 to 45
- hx_block: float32 [8, 262144], P(None, ('row', 'col')), may hold values from -120 to 120
- p_block: float32 [8, 262144], P(None, ('row', 'col')), may hold values from -6 to 6
- hp_block: float32 [8, 262144], P(None, ('row', 'col')), may hold values from -6 to 6
- tile_values: bfloat16 [8192, 256, 256], P(('row', 'col')), may hold values from -0.125 to 0.125
- tile_rows: int32 [8192], P(('row', 'col')), may hold values from 0 to 31, as said below
- tile_cols: int32 [8192], P(('row', 'col')), may hold values from 0 to 31, as said below
- tile_count: int32 [1024], P(('row', 'col')), may hold values from 1 to 8, as said below
- coeffs: float32 [24, 8], replicated, may hold values from -3 to 3
Outputs:
- gram_h: float32 [24, 24], replicated
- gram_s: float32 [24, 24], replicated
- x_next: float32 [8, 262144], P(None, ('row', 'col'))
- hx_next: float32 [8, 262144], P(None, ('row', 'col'))
Inputs may be any that keep to these rules, and one draw needn't show every extreme that they name: `tile_rows`: local tile row within the 32 tile rows of the device's grid row; the tile lies on or below the global diagonal. `tile_cols`: local tile column within the 32 tile columns of the device's grid column. `tile_count`: some device of the last grid row holds 8 live slots.
All inputs are finite; a program needn't handle non-finite values.
Results may differ from a plain program's by a relative error of at most 0.0012.
Values may be sent and summed in bfloat16 or wider, within the bound.
A program may use at most 32 MiB of HBM per device.

v0:
```python
import jax
import jax.numpy as jnp
from jax import lax
from jax.sharding import PartitionSpec as P


def tile_terms(tile_block, by_cols, by_rows, onehot_rows, onehot_cols, weight):
    highest = lax.Precision.HIGHEST
    forward = (
        jnp.einsum("sij,skj->ski", tile_block, by_cols, preferred_element_type=jnp.float32)
        * weight[:, None, None]
    )
    mirror = (
        jnp.einsum("sij,ski->skj", tile_block, by_rows, preferred_element_type=jnp.float32)
        * weight[:, None, None]
    )
    return (
        jnp.einsum("sr,ski->rki", onehot_rows, forward, precision=highest),
        jnp.einsum("sc,ski->cki", onehot_cols, mirror, precision=highest),
    )


def body(
    x_block, hx_block, p_block, hp_block, tile_values, tile_rows, tile_cols, tile_count, coeffs
):
    highest = lax.Precision.HIGHEST
    states = x_block.shape[0]
    shard_len = x_block.shape[1]
    tile_len = tile_values.shape[1]
    slot_count = tile_values.shape[0]
    cell_count = shard_len * lax.axis_size("row") * lax.axis_size("col")
    cross_sum, square = lax.psum(
        (jnp.sum(x_block * hx_block, axis=1), jnp.sum(x_block * x_block, axis=1)), ("row", "col")
    )
    theta_vals = cross_sum / square
    residual = hx_block - theta_vals[:, None] * x_block
    resid_half = residual.astype(jnp.bfloat16)
    col_group = lax.all_gather(resid_half, "row", axis=1, tiled=True)
    row_group = lax.all_gather(resid_half, "col", axis=1, tiled=True)
    col_tiles = col_group.reshape(states, -1, tile_len).transpose(1, 0, 2)
    row_tiles = row_group.reshape(states, -1, tile_len).transpose(1, 0, 2)
    picked_cols = jnp.take(col_tiles, tile_cols, axis=0)
    picked_rows = jnp.take(row_tiles, tile_rows, axis=0)
    live_mask = (jnp.arange(slot_count) < tile_count[0]).astype(jnp.float32)
    row_onehot = (tile_rows[:, None] == jnp.arange(row_tiles.shape[0])[None, :]).astype(jnp.float32)
    col_onehot = (tile_cols[:, None] == jnp.arange(col_tiles.shape[0])[None, :]).astype(jnp.float32)
    row_part, col_part = tile_terms(
        tile_values, picked_cols, picked_rows, row_onehot, col_onehot, live_mask
    )
    row_share = lax.psum_scatter(row_part, "col", scatter_dimension=0, tiled=True)
    col_share = lax.psum_scatter(col_part, "row", scatter_dimension=0, tiled=True)
    image = (row_share + col_share).transpose(1, 0, 2).reshape(states, shard_len)
    basis = jnp.concatenate([x_block, residual, p_block], axis=0)
    basis_image = jnp.concatenate([hx_block, image, hp_block], axis=0)
    gram_h, gram_s = lax.psum(
        (
            jnp.dot(basis, basis_image.T, precision=highest),
            jnp.dot(basis, basis.T, precision=highest),
        ),
        ("row", "col"),
    )
    gram_h = gram_h / cell_count
    gram_s = gram_s / cell_count
    x_next = jnp.dot(coeffs.T, basis, precision=highest)
    hx_next = jnp.dot(coeffs.T, basis_image, precision=highest)
    return (gram_h, gram_s, x_next, hx_next)


def solution(mesh):
    return jax.shard_map(
        body,
        mesh=mesh,
        in_specs=(
            P(None, ("row", "col")),
            P(None, ("row", "col")),
            P(None, ("row", "col")),
            P(None, ("row", "col")),
            P(("row", "col"), None, None),
            P(("row", "col")),
            P(("row", "col")),
            P(("row", "col")),
            P(),
        ),
        out_specs=(P(), P(), P(None, ("row", "col")), P(None, ("row", "col"))),
        check_vma=False,
    )
```

profile of v0, /device:TPU:1, one launch (start us, length us, event | category | flops | bytes accessed | tf_op | source)
XLA Modules:
  0.0 643.5 jit_solution(10830050626552773642)
XLA Ops:
  7.2 0.0 copy-start
  7.2 0.0 copy-start.7
  7.2 0.0 reduce-scatter.3.cloned.1.call-start
  7.2 0.7 compare_select_fusion.1
  8.0 0.0 copy-done.7
  8.0 0.0 copy-start.2
  8.0 0.9 multiply_reduce_fusion
  8.9 0.0 copy-start.1
  8.9 128.6 %all-reduce.1 = (f32[8]{0:T(128)S(1)}, f32[8]{0:T(128)S(1)}) all-reduce(f32[8]{0:T(128)S(1)} %get-tuple-element.6, f32[8]{0:T(128)S(1)} %get-tuple-element.5), channel_id=1, replica_groups=mesh['row'=32,'col'=32] {'row','col'}, use_global_device_ids=true, to_apply=%region_1.0 | all-reduce | flops 16 | bytes 128 | tf_op jit(solution)/shard_map/psum | solution.py:32
  137.5 0.0 copy-done.2
  137.5 0.0 copy-done.1
  137.5 0.1 fusion.26
  137.6 33.4 %all_gather.6 = bf16[8,8192]{1,0:T(8,128)(2,1)S(1)} all-gather(bf16[8,256]{1,0:T(8,128)(2,1)S(1)} %get-tuple-element.11), channel_id=1, replica_groups=mesh['row'=32,'col'=32] {'row'}, dimensions={1}, use_global_device_ids=true | all-gather | bytes 135168 | tf_op jit(solution)/shard_map/all_gather | solution.py:38
  171.7 0.6 gather_fusion
  172.2 0.0 copy-done
  172.3 0.0 copy-start.6
  172.3 0.4 fusion.4
  172.6 0.3 copy-done.6
  172.9 0.4 fusion.1
  173.3 0.8 copy.13
  174.1 0.0 reduce-scatter.3.cloned.1.call-update
  174.2 0.0 reduce-scatter.5.cloned.1.call-start
  174.2 64.8 %all_gather.7 = bf16[8,8192]{1,0:T(8,128)(2,1)S(1)} all-gather(bf16[8,256]{1,0:T(8,128)(2,1)S(1)} %get-tuple-element.11), channel_id=1, replica_groups=mesh['row'=32,'col'=32] {'col'}, dimensions={1}, use_global_device_ids=true | all-gather | bytes 135168 | tf_op jit(solution)/shard_map/all_gather | solution.py:39
  239.0 0.5 gather_fusion.1
  239.6 0.3 fusion.2
  239.9 0.4 fusion
  240.3 0.8 copy.14
  241.1 0.0 copy-start.3
  241.1 0.0 reduce-scatter.5.cloned.1.call-update
  241.1 0.7 copy-done.3
  241.8 0.0 copy-start.5
  241.8 0.1 fusion.13
  242.0 0.5 copy-done.5
  242.5 0.7 convolution_bitcast_fusion.1
  243.2 0.0 copy-start.4
  243.2 151.0 %reduce-scatter.3.cloned.1.call-done = f32[1,8,256]{2,1,0:T(8,128)} async-done(((f32[32,8,256]{2,1,0:T(8,128)}), f32[1,8,256]{2,1,0:T(8,128)}) %reduce-scatter.3.cloned.1.call-update) | async-done | bytes 8208 | tf_op jit(solution)/shard_map/reduce_scatter | solution.py:50
  394.2 123.9 %reduce-scatter.5.cloned.1.call-done = f32[1,8,256]{2,1,0:T(8,128)} async-done(((f32[32,8,256]{2,1,0:T(8,128)}), f32[1,8,256]{2,1,0:T(8,128)}) %reduce-scatter.5.cloned.1.call-update) | async-done | bytes 8208 | tf_op jit(solution)/shard_map/reduce_scatter | solution.py:51
  518.2 0.7 add_bitcast_fusion
  518.9 0.0 copy-done.4
  518.9 0.1 fusion.10
  519.0 0.7 convolution_bitcast_fusion
  519.8 116.3 %all-reduce = (f32[24,24]{1,0:T(8,128)S(1)}, f32[24,24]{1,0:T(8,128)S(1)}) all-reduce(f32[24,24]{1,0:T(8,128)S(1)} %fusion.10, f32[24,24]{1,0:T(8,128)S(1)} %fusion.13), channel_id=1, replica_groups=mesh['row'=32,'col'=32] {'row','col'}, use_global_device_ids=true, to_apply=%region_6.8 | all-reduce | flops 1152 | bytes 9216 | tf_op jit(solution)/shard_map/psum | solution.py:55
  636.0 0.6 broadcast_multiply_fusion
  (7 shorter events, 0.0 us)
Async XLA Ops:
  7.2 165.1 %copy-start = (bf16[8,256,256]{2,1,0:T(8,128)(2,1)S(1)}, bf16[8,256,256]{2,1,0:T(8,128)(2,1)}, u32[]{:S(2)}) copy-start(bf16[8,256,256]{2,1,0:T(8,128)(2,1)} %param.15) | copy-start | bytes 3145732
  7.2 0.8 copy-start.7
  7.2 387.1 %reduce-scatter.3.cloned.1.call-start = ((), (), s32[]{:S(2)}) async-start(), calls=%async_computation.2 | async-start | bytes 270336 | tf_op jit(solution)/shard_map/reduce_scatter | solution.py:50
  8.0 129.5 %copy-start.2 = (f32[8,256]{1,0:T(8,128)S(1)}, f32[8,256]{1,0:T(8,128)}, u32[]{:S(2)}) copy-start(f32[8,256]{1,0:T(8,128)} %param.12) | copy-start | bytes 24580
  8.9 128.6 %copy-start.1 = (f32[8,256]{1,0:T(8,128)S(1)}, f32[8,256]{1,0:T(8,128)}, u32[]{:S(2)}) copy-start(f32[8,256]{1,0:T(8,128)} %param.11) | copy-start | bytes 24580
  172.3 0.7 copy-start.6
  174.2 344.0 %reduce-scatter.5.cloned.1.call-start = ((), (), s32[]{:S(2)}) async-start(), calls=%async_computation.3 | async-start | bytes 270336 | tf_op jit(solution)/shard_map/reduce_scatter | solution.py:51
  241.1 0.7 copy-start.3
  241.8 0.7 copy-start.5
  243.2 275.7 %copy-start.4 = (f32[8,256]{1,0:T(8,128)S(1)}, f32[8,256]{1,0:T(8,128)}, u32[]{:S(2)}) copy-start(f32[8,256]{1,0:T(8,128)} %param.14) | copy-start | bytes 24580
Sparse Core Ops, SparseCore 0:
  174.3 219.9 reduce-scatter.2
  398.0 120.1 reduce-scatter.4
where the time goes:
time: 644 us; the launch traced here: 643 us
  blocking collectives  343 us (53%)
  waiting for transfers between devices  275 us (43%)
  between operations  14.8 us (2%)
    reduce_scatter x1, waiting for transfers between devices, body(): lax.psum_scatter(row_part, 'col', scatter_dimension=0, tiled=True)  151 us
    psum x1, blocking collectives, body(): lax.psum((jnp.sum(x_block * hx_block, axis=1), jnp.sum(x_block * x_block,...  129 us
    reduce_scatter x1, waiting for transfers between devices, body(): lax.psum_scatter(col_part, 'row', scatter_dimension=0, tiled=True)  124 us
    psum x1, blocking collectives, body(): lax.psum((jnp.dot(basis, basis_image.T, precision=highest), jnp.dot(basis...  116 us
    all_gather x1, blocking collectives, body(): row_group = lax.all_gather(resid_half, 'col', axis=1, tiled=True)  64.8 us
    all_gather x1, blocking collectives, body(): col_group = lax.all_gather(resid_half, 'row', axis=1, tiled=True)  33.4 us
  transfers between devices with their start and end apart: 2, of which 2 were waited for; matrix products, arithmetic and copies ran while one was open for 0% of the time, Pallas kernels for 0%

commit v1 on v0

v1 whole, which is shorter than its diff:
```python
import functools

import jax
import jax.numpy as jnp
from jax import lax
from jax.experimental import pallas as pl
from jax.experimental.pallas import tpu as pltpu
from jax.sharding import PartitionSpec as P

MESH = pl.DeviceIdType.MESH
F32 = jnp.float32
BF16 = jnp.bfloat16
EXACT = lax.Precision.HIGHEST
LEVELS = 32767.0
NT = (((1,), (1,)), ((), ()))
NN = (((1,), (0,)), ((), ()))
TN = (((0,), (0,)), ((), ()))


def iota(shape, axis):
    return lax.broadcasted_iota(jnp.int32, shape, axis)


def dot(a, b, dims, precision=None):
    return lax.dot_general(a, b, dims, precision=precision, preferred_element_type=F32)


def to_row(columns):
    lane, sub = iota((8, 128), 1), iota((8, 128), 0)
    total = jnp.zeros((8, 128), F32)
    for place, column in enumerate(columns):
        total = total + jnp.where(lane == sub + 8 * place, column, 0.0)
    return jnp.sum(total, axis=0, keepdims=True)


def from_row(row, place):
    lane, sub = iota((8, 128), 1), iota((8, 128), 0)
    return jnp.sum(jnp.where(lane == sub + 8 * place, row, 0.0), axis=1, keepdims=True)


def halves(v):
    return v[:, :128], v[:, 128:]


def coded(v):
    top = jnp.max(jnp.abs(v), axis=1, keepdims=True)
    usable = top > 1e-30
    inverse = jnp.where(usable, LEVELS / jnp.where(usable, top, 1.0), 0.0)
    return jnp.round(v * inverse), top * (1.0 / LEVELS)


def split(v):
    high = v.astype(BF16)
    return high, (v - high.astype(F32)).astype(BF16)


def wait(ref, sem):
    pltpu.make_async_copy(ref, ref, sem).wait()


def kernel(
    rows_n, cols_n, cells, slots,
    x_ref, hx_ref, p_ref, hp_ref, tiles_hbm, rows_ref, cols_ref, count_ref, coef_ref,
    xn_ref, hxn_ref, gh_ref, gs_ref,
    tiles, stat, rstat, cstat, csum, csums, bundle, rbun, cbun,
    early, erow, esum, ecol, late, lrow, lsum, lcol, rsend, csend, rrecv, crecv,
    tile_sem, send, recv,
):
    r, c = lax.axis_index("row"), lax.axis_index("col")

    def along_col(i):
        return lax.rem(c + 1 + i, cols_n)

    def along_row(i):
        return lax.rem(r + 1 + i, rows_n)

    def each(n, f):
        def step(i, carry):
            f(i)
            return carry
        lax.fori_loop(0, n - 1, step, 0)

    def push(src, dst, k, axis, j):
        pltpu.make_async_remote_copy(
            src_ref=src, dst_ref=dst, send_sem=send.at[k], recv_sem=recv.at[k],
            device_id={axis: j}, device_id_type=MESH,
        ).start()

    barrier = pltpu.get_barrier_semaphore()
    each(cols_n, lambda i: pl.semaphore_signal(
        barrier, inc=1, device_id={"col": along_col(i)}, device_id_type=MESH))
    each(rows_n, lambda i: pl.semaphore_signal(
        barrier, inc=1, device_id={"row": along_row(i)}, device_id_type=MESH))
    tile_copy = pltpu.make_async_copy(tiles_hbm, tiles, tile_sem)
    tile_copy.start()

    x, hx, p, hp = x_ref[...], hx_ref[...], p_ref[...], hp_ref[...]
    cross = jnp.sum(x * hx, axis=1, keepdims=True)
    square = jnp.sum(x * x, axis=1, keepdims=True)
    some = square > 0.0
    guess = jnp.where(some, cross / jnp.where(some, square, 1.0), 0.0)
    near = hx - guess * x
    near_code, near_step = coded(near)
    x_code, x_step = coded(x)
    p_code, p_step = coded(p)
    row = to_row([cross, square, guess, near_step, x_step, p_step])
    stat[...] = row
    rstat[c] = row
    cstat[r] = row
    (nl, nh), (xl, xh), (pl_, ph) = halves(near_code), halves(x_code), halves(p_code)
    packed = jnp.concatenate([nl, xl, nh, xh, pl_, ph], axis=0).astype(jnp.int32).astype(jnp.int16)
    bundle[...] = packed
    rbun[c] = packed
    cbun[r] = packed

    pl.semaphore_wait(barrier, rows_n + cols_n - 2)

    each(cols_n, lambda i: push(stat, rstat.at[c], 0, "col", along_col(i)))
    each(rows_n, lambda i: push(stat, cstat.at[r], 1, "row", along_row(i)))

    def push_bundle(i):
        push(bundle, rbun.at[c], 2, "col", along_col(i))
        push(bundle, cbun.at[r], 3, "row", along_row(i))

    if rows_n == cols_n:
        each(cols_n, push_bundle)

    lane, sub = iota((8, 128), 1), iota((8, 128), 0)
    own_state = lax.rem(lane, 8) == sub
    slot_of = lax.rem(lane, 8 * slots) // 8

    def onehot(ids, n):
        place = jnp.zeros((8, 128), jnp.int32)
        for s in range(slots):
            place = jnp.where(slot_of == s, ids[s], place)
        blocks = [jnp.where((place == d) & own_state, 1.0, 0.0) for d in range(n)]
        return jnp.concatenate(blocks, axis=0).astype(BF16)

    row_hot, col_hot = onehot(rows_ref, cols_n), onehot(cols_ref, rows_n)

    wait(rstat.at[pl.ds(0, cols_n - 1)], recv.at[0])
    col_total = jnp.sum(rstat[...], axis=0)
    csum[...] = col_total
    csums[r] = col_total
    each(rows_n, lambda i: push(csum, csums.at[r], 4, "row", along_row(i)))
    wait(csums.at[pl.ds(0, rows_n - 1)], recv.at[4])
    total = jnp.sum(csums[...], axis=0)
    theta = from_row(total, 0) / from_row(total, 1)
    residual = hx - theta * x

    basis = jnp.concatenate([x, residual, p], axis=0)
    others = jnp.concatenate([basis, hx, hp, jnp.zeros((88, x.shape[1]), F32)], axis=0)
    products = dot(basis, others, NT, EXACT)
    tile = (products[0:8] + pltpu.roll(products[8:16], 40, 1)) + pltpu.roll(products[16:24], 80, 1)
    early[...] = tile
    erow[r] = tile
    each(rows_n, lambda i: push(early, erow.at[r], 5, "row", along_row(i)))

    wait(rbun.at[pl.ds(0, cols_n - 1)], recv.at[2])
    wait(cbun.at[pl.ds(0, rows_n - 1)], recv.at[3])
    wait(cstat.at[pl.ds(0, rows_n - 1)], recv.at[1])
    tile_copy.wait()

    def fetch(stats, shards, at):
        numbers = stats[at]
        code = shards[at].astype(jnp.int32).astype(F32)
        near_part = from_row(numbers, 3)
        x_part = from_row(numbers, 4)
        p_part = from_row(numbers, 5)
        shift = (from_row(numbers, 2) - theta) * x_part
        wide = lambda a, b: jnp.concatenate([code[a:a + 8], code[b:b + 8]], axis=1)
        x_wide = wide(8, 24)
        res = near_part * wide(0, 16) + shift * x_wide
        return res, jnp.concatenate([x_part * x_wide, res, p_part * wide(32, 40)], axis=0)

    forward, mirror = [], []
    partial = jnp.zeros((16, 48), F32)
    for s in range(slots):
        live = jnp.where(s < count_ref[0], 1.0, 0.0).astype(F32)
        by_col, col_basis = fetch(cstat, cbun, cols_ref[s])
        by_row, row_basis = fetch(rstat, rbun, rows_ref[s])
        matrix = tiles[s]
        f = dot(by_col.astype(BF16), matrix, NT) * live
        m = dot(by_row.astype(BF16), matrix, NN) * live
        fh, fl = split(f)
        mh, ml = split(m)
        forward.append((fh, fl))
        mirror.append((mh, ml))
        rb = jnp.concatenate(split(row_basis), axis=0)
        cb = jnp.concatenate(split(col_basis), axis=0)
        partial = partial + dot(jnp.concatenate([fh, fl], axis=0), rb, NT)
        partial = partial + dot(jnp.concatenate([mh, ml], axis=0), cb, NT)

    g = partial[0:8] + partial[8:16]
    from_lane = iota((48, 256), 0)
    to_lane = lax.rem(iota((48, 256), 1), 32)
    spread = jnp.where((from_lane == to_lane) & (to_lane < 24) | (from_lane == to_lane + 24) & (to_lane < 24), 1.0, 0.0)
    g = dot(g, spread, NN, EXACT)
    g = jnp.sum(jnp.where(iota((8, 256), 1) // 32 == iota((8, 256), 0), g, 0.0), axis=0, keepdims=True)
    flat = jnp.concatenate([g[:, :128], g[:, 128:]], axis=0)
    late[...] = flat
    lrow[r] = flat
    each(rows_n, lambda i: push(late, lrow.at[r], 7, "row", along_row(i)))

    def spread_out(hot, parts, n, buffer):
        stack = jnp.concatenate([h for h, _ in parts] + [l for _, l in parts], axis=0)
        out = dot(hot, stack, NN)
        left, right = halves(out)
        out = jnp.concatenate([left.reshape(n, 8, 128), right.reshape(n, 8, 128)], axis=1)
        buffer[...] = out.astype(BF16)

    spread_out(row_hot, forward, cols_n, rsend)
    spread_out(col_hot, mirror, rows_n, csend)

    def push_parts(i):
        j, k = along_col(i), along_row(i)
        push(rsend.at[j], rrecv.at[c], 9, "col", j)
        push(csend.at[k], crecv.at[r], 10, "row", k)

    if rows_n == cols_n:
        each(cols_n, push_parts)
    rrecv[c] = rsend[c]
    crecv[r] = csend[r]

    wait(erow.at[pl.ds(0, rows_n - 1)], recv.at[5])
    tile = jnp.sum(erow[...], axis=0)
    esum[...] = tile
    ecol[c] = tile
    each(cols_n, lambda i: push(esum, ecol.at[c], 6, "col", along_col(i)))

    wait(lrow.at[pl.ds(0, rows_n - 1)], recv.at[7])
    flat = jnp.sum(lrow[...], axis=0)
    lsum[...] = flat
    lcol[c] = flat
    each(cols_n, lambda i: push(lsum, lcol.at[c], 8, "col", along_col(i)))

    coef = coef_ref[...]
    xn_ref[...] = dot(coef, basis, TN, EXACT)

    wait(rrecv.at[pl.ds(0, cols_n - 1)], recv.at[9])
    wait(crecv.at[pl.ds(0, rows_n - 1)], recv.at[10])
    image = jnp.sum(rrecv[...].astype(F32), axis=0) + jnp.sum(crecv[...].astype(F32), axis=0)
    image = jnp.concatenate([image[0:8], image[8:16]], axis=1)
    hxn_ref[...] = dot(coef, jnp.concatenate([hx, image, hp], axis=0), TN, EXACT)

    scale = 1.0 / cells
    wait(ecol.at[pl.ds(0, cols_n - 1)], recv.at[6])
    tile = jnp.sum(ecol[...], axis=0)
    products = jnp.concatenate([tile, pltpu.roll(tile, 88, 1), pltpu.roll(tile, 48, 1)], axis=0) * scale
    gs_ref[...] = products[:, :24]

    wait(lcol.at[pl.ds(0, cols_n - 1)], recv.at[8])
    flat = jnp.sum(lcol[...], axis=0)
    flat = jnp.concatenate([flat[0:1], flat[1:2]], axis=1)
    mine = lax.rem(iota((24, 256), 1), 32) == iota((24, 256), 0)
    gather = jnp.where(iota((256, 128), 1) == 8 + iota((256, 128), 0) // 32, scale, 0.0)
    middle = dot(jnp.where(mine, flat, 0.0), gather, NN, EXACT)
    at = iota((24, 128), 1)
    full = jnp.where(at < 8, pltpu.roll(products, 104, 1), jnp.where(at < 16, middle, pltpu.roll(products, 112, 1)))
    gh_ref[...] = full[:, :24]

    for k, ref, n in ((0, rstat, cols_n), (1, cstat, rows_n), (2, rbun, cols_n), (3, cbun, rows_n),
                      (4, csums, rows_n), (5, erow, rows_n), (6, ecol, cols_n), (7, lrow, rows_n),
                      (8, lcol, cols_n), (9, rrecv, cols_n), (10, crecv, rows_n)):
        wait(ref.at[pl.ds(0, n - 1)], send.at[k])


def body(x_block, hx_block, p_block, hp_block, tile_values, tile_rows, tile_cols, tile_count, coeffs):
    rows_n, cols_n = lax.axis_size("row"), lax.axis_size("col")
    states, length = x_block.shape
    slots = tile_values.shape[0]
    vmem = pl.BlockSpec(memory_space=pltpu.VMEM)
    smem = pl.BlockSpec(memory_space=pltpu.SMEM)
    small, big, word = pltpu.VMEM, pltpu.VMEM, jnp.int16
    gh, gs, xn, hxn = (2, 3, 0, 1)
    outs = pl.pallas_call(
        functools.partial(kernel, rows_n, cols_n, length * rows_n * cols_n, slots),
        out_shape=(
            jax.ShapeDtypeStruct((states, length), F32),
            jax.ShapeDtypeStruct((states, length), F32),
            jax.ShapeDtypeStruct((24, 24), F32),
            jax.ShapeDtypeStruct((24, 24), F32),
        ),
        in_specs=[vmem] * 4 + [pl.BlockSpec(memory_space=pltpu.HBM)] + [smem] * 3 + [vmem],
        out_specs=(vmem,) * 4,
        scratch_shapes=[
            pltpu.VMEM(tile_values.shape, BF16),
            pltpu.VMEM((1, 128), F32),
            pltpu.VMEM((cols_n, 1, 128), F32),
            pltpu.VMEM((rows_n, 1, 128), F32),
            pltpu.VMEM((1, 128), F32),
            pltpu.VMEM((rows_n, 1, 128), F32),
            pltpu.VMEM((48, 128), word),
            pltpu.VMEM((cols_n, 48, 128), word),
            pltpu.VMEM((rows_n, 48, 128), word),
            pltpu.VMEM((8, 128), F32),
            pltpu.VMEM((rows_n, 8, 128), F32),
            pltpu.VMEM((8, 128), F32),
            pltpu.VMEM((cols_n, 8, 128), F32),
            pltpu.VMEM((2, 128), F32),
            pltpu.VMEM((rows_n, 2, 128), F32),
            pltpu.VMEM((2, 128), F32),
            pltpu.VMEM((cols_n, 2, 128), F32),
            pltpu.VMEM((cols_n, 16, 128), BF16),
            pltpu.VMEM((rows_n, 16, 128), BF16),
            pltpu.VMEM((cols_n, 16, 128), BF16),
            pltpu.VMEM((rows_n, 16, 128), BF16),
            pltpu.SemaphoreType.DMA,
            pltpu.SemaphoreType.DMA((11,)),
            pltpu.SemaphoreType.DMA((11,)),
        ],
        compiler_params=pltpu.CompilerParams(
            collective_id=0, has_side_effects=True, vmem_limit_bytes=32 << 20
        ),
        name="step",
    )(x_block, hx_block, p_block, hp_block, tile_values, tile_rows, tile_cols, tile_count, coeffs)
    return outs[gh], outs[gs], outs[xn], outs[hxn]


def solution(mesh):
    both = ("row", "col")
    return jax.shard_map(
        body,
        mesh=mesh,
        in_specs=(
            P(None, both), P(None, both), P(None, both), P(None, both),
            P(both, None, None), P(both), P(both), P(both), P(),
        ),
        out_specs=(P(), P(), P(None, both), P(None, both)),
        check_vma=False,
    )
```

time: 644 us -> 67.1 us (0.10)
  blocking collectives: 343 us -> 0 us
  waiting for transfers between devices: 275 us -> 0 us
  Pallas kernels: 0 us -> 59.6 us
  between operations: 14.8 us -> 1.36 us
    reduce_scatter x2 -> x0, waiting for transfers between devices: 275 us -> none  [the longest x1 151 us: body(): lax.psum_scatter(row_part, 'col', scatter_dimension=0, tiled=True)]
    psum x2 -> x0, blocking collectives: 245 us -> none  [the longest x1 129 us: body(): lax.psum((jnp.sum(x_block * hx_block, axis=1), jnp.sum(x_block * x_block,...]
    all_gather x2 -> x0, blocking collectives: 98.2 us -> none  [the longest x1 64.8 us: body(): row_group = lax.all_gather(resid_half, 'col', axis=1, tiled=True)]
    pallas_call x0 -> x1, Pallas kernels: none -> 59.6 us  [body(): pl.pallas_call(functools.partial(kernel, rows_n, cols_n, length * rows_n...]
  transfers between devices with their start and end apart: 2 -> 0, of which waited for: 2 -> 0; matrix products, arithmetic and copies ran while one was open for 0% -> 0% of each run, Pallas kernels for 0% -> 0%
where the time goes in v1:
time: 67.1 us; the launch traced here: 66.8 us
  Pallas kernels  59.6 us (89%)
  local copies, waits for them, and re-layouts  5.8 us (9%)
  between operations  1.36 us (2%)
    pallas_call x1, Pallas kernels, body(): pl.pallas_call(functools.partial(kernel, rows_n, cols_n, length * rows_n...  59.6 us
    unnamed x19, local copies, waits for them, and re-layouts  5.8 us

profile of v1, /device:TPU:1, one launch (start us, length us, event | category | flops | bytes accessed | tf_op | source)
XLA Modules:
  0.0 66.8 jit_solution(15160510923834707917)
XLA Ops:
  0.6 0.0 copy-start.5
  0.6 0.0 copy-start.6
  1.3 0.0 copy-start.1
  1.3 0.0 copy-start.2
  1.3 0.8 %copy.13.coef_ref = f32[24,8]{1,0:T(8,128)S(1)} copy(f32[24,8]{0,1:T(8,128)} %param.17) | data formatting | bytes 1536 | tf_op args[8]
  2.1 0.0 copy-done.5
  2.1 0.0 copy-done.6
  2.1 0.0 copy-done.1
  2.1 0.0 copy-done.2
  2.1 0.0 copy-start
  2.1 1.2 %copy-done = bf16[8,256,256]{2,1,0:T(8,128)(2,1)S(1)} copy-done((bf16[8,256,256]{2,1,0:T(8,128)(2,1)S(1)}, bf16[8,256,256]{2,1,0:T(8,128)(2,1)}, u32[]{:S(2)}) %copy-start) | copy-done | bytes 1048600
  3.4 0.0 copy-start.3
  3.4 0.7 %copy-done.3 = f32[8,256]{1,0:T(8,128)S(1)} copy-done((f32[8,256]{1,0:T(8,128)S(1)}, f32[8,256]{1,0:T(8,128)}, u32[]{:S(2)}) %copy-start.3) | copy-done | bytes 8216
  4.1 0.0 copy-start.4
  4.1 0.7 %copy-done.4 = f32[8,256]{1,0:T(8,128)S(1)} copy-done((f32[8,256]{1,0:T(8,128)S(1)}, f32[8,256]{1,0:T(8,128)}, u32[]{:S(2)}) %copy-start.4) | copy-done | bytes 8216
  4.8 59.6 %step.1 = (f32[8,256]{1,0:T(8,128)S(1)}, f32[8,256]{1,0:T(8,128)S(1)}, f32[24,24]{1,0:T(8,128)S(1)}, f32[24,24]{1,0:T(8,128)S(1)}) custom-call(f32[8,256]{1,0:T(8,128)S(1)} %copy-done.1, f32[8,256]{1,0:T(8,128)S(1)} %copy-done.2, f32[8,256]{1,0:T(8,128)S(1)} %copy-done.3, f32[8,256]{1,0:T(8,128)S(1)} %copy-done.4, bf16[8,256,256]{2,1,0:T(8,128)(2,1)S(1)} %copy-done, ...), custom_call_target="tpu_custom_call" | custom-call | tf_op jit(solution)/shard_map/step/pallas_call | solution.py:276
  64.4 0.6 copy.19
  65.0 0.6 copy.20
  65.6 0.6 copy.21
  66.2 0.6 copy.22
Async XLA Ops:
  0.6 1.5 %copy-start.5 = (s32[8]{0:T(128)S(1)}, s32[8]{0:T(128)}, u32[]{:S(2)}) copy-start(s32[8]{0:T(128)} %rows_ref.1) | copy-start | bytes 100
  0.6 1.5 %copy-start.6 = (s32[8]{0:T(128)S(1)}, s32[8]{0:T(128)}, u32[]{:S(2)}) copy-start(s32[8]{0:T(128)} %cols_ref.1) | copy-start | bytes 100
  1.3 0.8 %copy-start.1 = (f32[8,256]{1,0:T(8,128)S(1)}, f32[8,256]{1,0:T(8,128)}, u32[]{:S(2)}) copy-start(f32[8,256]{1,0:T(8,128)} %x_ref.1) | copy-start | bytes 24580
  1.3 0.8 %copy-start.2 = (f32[8,256]{1,0:T(8,128)S(1)}, f32[8,256]{1,0:T(8,128)}, u32[]{:S(2)}) copy-start(f32[8,256]{1,0:T(8,128)} %hx_ref.1) | copy-start | bytes 24580
  2.1 1.2 %copy-start = (bf16[8,256,256]{2,1,0:T(8,128)(2,1)S(1)}, bf16[8,256,256]{2,1,0:T(8,128)(2,1)}, u32[]{:S(2)}) copy-start(bf16[8,256,256]{2,1,0:T(8,128)(2,1)} %tiles_hbm.1) | copy-start | bytes 3145732
  3.4 0.7 %copy-start.3 = (f32[8,256]{1,0:T(8,128)S(1)}, f32[8,256]{1,0:T(8,128)}, u32[]{:S(2)}) copy-start(f32[8,256]{1,0:T(8,128)} %p_ref.1) | copy-start | bytes 24580
  4.1 0.7 %copy-start.4 = (f32[8,256]{1,0:T(8,128)S(1)}, f32[8,256]{1,0:T(8,128)}, u32[]{:S(2)}) copy-start(f32[8,256]{1,0:T(8,128)} %hp_ref.1) | copy-start | bytes 24580

commit v2 on v1

v2 whole, which is shorter than its diff:
```python
import functools

import jax
import jax.numpy as jnp
from jax import lax
from jax.experimental import pallas as pl
from jax.experimental.pallas import tpu as pltpu
from jax.sharding import PartitionSpec as P

MESH = pl.DeviceIdType.MESH
F32 = jnp.float32
BF16 = jnp.bfloat16
EXACT = lax.Precision.HIGHEST
LEVELS = 32767.0
LIMIT = 60 << 20
NT = (((1,), (1,)), ((), ()))
NN = (((1,), (0,)), ((), ()))


def iota(shape, axis):
    return lax.broadcasted_iota(jnp.int32, shape, axis)


def dot(a, b, dims, precision=None):
    return lax.dot_general(a, b, dims, precision=precision, preferred_element_type=F32)


def to_row(columns):
    lane, sub = iota((8, 128), 1), iota((8, 128), 0)
    total = jnp.zeros((8, 128), F32)
    for place, column in enumerate(columns):
        total = total + jnp.where(lane == sub + 8 * place, column, 0.0)
    return jnp.sum(total, axis=0, keepdims=True)


def from_row(row, place):
    lane, sub = iota((8, 128), 1), iota((8, 128), 0)
    return jnp.sum(jnp.where(lane == sub + 8 * place, row, 0.0), axis=1, keepdims=True)


def halves(v):
    return v[:, :128], v[:, 128:]


def coded(v):
    top = jnp.max(jnp.abs(v), axis=1, keepdims=True)
    usable = top > 1e-30
    inverse = jnp.where(usable, LEVELS / jnp.where(usable, top, 1.0), 0.0)
    return jnp.round(v * inverse), top * (1.0 / LEVELS)


def split(v):
    high = v.astype(BF16)
    return high, (v - high.astype(F32)).astype(BF16)


def wait(ref, sem):
    pltpu.make_async_copy(ref, ref, sem).wait()


def near_of(n):
    return 4 if n >= 16 else 2


def kernel(
    rows_n, cols_n, cells, slots,
    x_hbm, hx_hbm, p_hbm, hp_hbm, tiles_hbm, rows_hbm, cols_hbm, count_hbm, coef_hbm,
    xn_ref, hxn_ref, gh_ref, gs_ref,
    x_ref, hx_ref, p_ref, hp_ref, tiles, rows_ref, cols_ref, count_ref, coef_ref,
    stat, rstat, cstat, csum, csums, near_send, rnear, cnear, pair_send, rpair, cpair,
    early, early_x, early_q, early_h, early_z, late, lrow, lsum, lcol, rsend, csend, rrecv, crecv,
    load, send, recv,
):
    r, c = lax.axis_index("row"), lax.axis_index("col")
    near_n, high_n = near_of(rows_n), near_of(cols_n)
    x_n, z_n = rows_n // near_n, cols_n // high_n
    my_x, my_q = r // near_n, lax.rem(r, near_n)
    my_h, my_z = c // z_n, lax.rem(c, z_n)
    my_slot = my_z * high_n + my_h
    my_near = my_q * x_n + my_x

    def along_col(i):
        return lax.rem(c + 1 + i, cols_n)

    def along_row(i):
        return lax.rem(r + 1 + i, rows_n)

    def each(n, f):
        def step(i, carry):
            f(i)
            return carry
        lax.fori_loop(0, n - 1, step, 0)

    def push(src, dst, k, axis, j):
        pltpu.make_async_remote_copy(
            src_ref=src, dst_ref=dst, send_sem=send.at[k], recv_sem=recv.at[k],
            device_id={axis: j}, device_id_type=MESH,
        ).start()

    table = (
        (0, rstat, cols_n - 1), (1, cstat, rows_n - 1), (4, csums, rows_n - 1),
        (5, cpair, near_n - 1), (13, cpair, rows_n - near_n), (6, rpair, high_n - 1), (14, rpair, cols_n - high_n),
        (3, cnear, x_n - 1), (18, cnear, rows_n - x_n), (2, rnear, z_n - 1), (17, rnear, cols_n - z_n),
        (16, early_z, z_n - 1), (15, early_h, high_n - 1), (11, early_x, x_n - 1), (12, early_q, near_n - 1),
        (7, lrow, rows_n - 1), (8, lcol, cols_n - 1), (9, rrecv, cols_n - 1), (10, crecv, rows_n - 1),
    )

    def arrive(k):
        ref, n = next((ref, n) for j, ref, n in table if j == k)
        wait(ref.at[pl.ds(0, n)], recv.at[k])

    loads = [
        pltpu.make_async_copy(a, b, load.at[k])
        for k, (a, b) in enumerate((
            (x_hbm, x_ref), (hx_hbm, hx_ref), (p_hbm, p_ref), (hp_hbm, hp_ref), (tiles_hbm, tiles),
            (rows_hbm, rows_ref), (cols_hbm, cols_ref), (count_hbm, count_ref), (coef_hbm, coef_ref)))
    ]
    for copy in loads:
        copy.start()
    barrier = pltpu.get_barrier_semaphore()
    each(cols_n, lambda i: pl.semaphore_signal(
        barrier, inc=1, device_id={"col": along_col(i)}, device_id_type=MESH))
    each(rows_n, lambda i: pl.semaphore_signal(
        barrier, inc=1, device_id={"row": along_row(i)}, device_id_type=MESH))
    for k in (0, 1, 2, 3, 5, 6, 7, 8):
        loads[k].wait()

    x, hx, p, hp = x_ref[...], hx_ref[...], p_ref[...], hp_ref[...]
    cross = jnp.sum(x * hx, axis=1, keepdims=True)
    square = jnp.sum(x * x, axis=1, keepdims=True)
    some = square > 0.0
    guess = jnp.where(some, cross / jnp.where(some, square, 1.0), 0.0)
    near = hx - guess * x
    near_code, near_step = coded(near)
    x_code, x_step = coded(x)
    p_code, p_step = coded(p)
    row = to_row([cross, square, guess, near_step, x_step, p_step])
    stat[...] = row
    rstat[c] = row
    cstat[r] = row
    near_code = jnp.concatenate(halves(near_code), axis=0).astype(jnp.int32).astype(jnp.int16)
    near_send[...] = near_code
    rnear[c] = near_code
    cnear[my_near] = near_code
    pair = jnp.concatenate(halves(x_code) + halves(p_code), axis=0).astype(jnp.int32).astype(jnp.int16)
    pair_send[...] = pair
    rpair[my_slot] = pair
    cpair[r] = pair

    pl.semaphore_wait(barrier, rows_n + cols_n - 2)

    def offsets(n, f):
        for i in range(1, n):
            f(i)

    def at_x(i):
        return lax.rem(my_x + i, x_n) * near_n + my_q

    def at_q(i):
        return my_x * near_n + lax.rem(my_q + i, near_n)

    def at_z(i):
        return my_h * z_n + lax.rem(my_z + i, z_n)

    def at_h(i):
        return lax.rem(my_h + i, high_n) * z_n + my_z

    each(cols_n, lambda i: push(stat, rstat.at[c], 0, "col", along_col(i)))
    offsets(high_n, lambda i: push(pair_send, rpair.at[my_slot], 6, "col", at_h(i)))
    offsets(near_n, lambda i: push(pair_send, cpair.at[r], 5, "row", at_q(i)))
    offsets(z_n, lambda i: push(near_send, rnear.at[c], 2, "col", at_z(i)))
    offsets(x_n, lambda i: push(near_send, cnear.at[my_near], 3, "row", at_x(i)))
    each(rows_n, lambda i: push(stat, cstat.at[r], 1, "row", along_row(i)))

    lane, sub = iota((8, 128), 1), iota((8, 128), 0)
    own_state = lax.rem(lane, 8) == sub
    slot_of = lax.rem(lane, 8 * slots) // 8

    def onehot(ids, n):
        place = jnp.zeros((8, 128), jnp.int32)
        for s in range(slots):
            place = jnp.where(slot_of == s, ids[s], place)
        blocks = [jnp.where((place == d) & own_state, 1.0, 0.0) for d in range(n)]
        return jnp.concatenate(blocks, axis=0).astype(BF16)

    row_hot, col_hot = onehot(rows_ref, cols_n), onehot(cols_ref, rows_n)

    def onward(n, ref, first, size, k, axis, at):
        group = ref.at[pl.ds(first, size)]
        offsets(n, lambda i: push(group, group, k, axis, at(i)))

    arrive(5)
    onward(x_n, cpair, my_x * near_n, near_n, 13, "row", at_x)
    arrive(3)
    onward(near_n, cnear, my_q * x_n, x_n, 18, "row", at_q)
    arrive(6)
    onward(z_n, rpair, my_z * high_n, high_n, 14, "col", at_z)
    arrive(2)
    onward(high_n, rnear, my_h * z_n, z_n, 17, "col", at_h)

    arrive(0)
    col_total = jnp.sum(rstat[...], axis=0)
    csum[...] = col_total
    csums[r] = col_total
    each(rows_n, lambda i: push(csum, csums.at[r], 4, "row", along_row(i)))
    row_cross, row_square = from_row(col_total, 0), from_row(col_total, 1)
    some = row_square > 0.0
    row_theta = jnp.where(some, row_cross / jnp.where(some, row_square, 1.0), 0.0)
    basis = jnp.concatenate([x, hx - row_theta * x, p], axis=0)
    others = jnp.concatenate([basis, hx, hp, jnp.zeros((88, x.shape[1]), F32)], axis=0)
    products = dot(basis, others, NT, EXACT)
    tile = (products[0:8] + pltpu.roll(products[8:16], 40, 1)) + pltpu.roll(products[16:24], 80, 1)
    early[0] = tile
    early_z[my_z] = tile
    offsets(z_n, lambda i: push(early.at[0], early_z.at[my_z], 16, "col", at_z(i)))

    arrive(1)

    def numbers(row):
        return [from_row(row, place) for place in (2, 3, 4, 5)]

    col_numbers = [numbers(cstat[cols_ref[s]]) for s in range(slots)]
    row_numbers = [numbers(rstat[rows_ref[s]]) for s in range(slots)]

    def early_step(k, n, gathered):
        arrive(k)
        return jnp.sum(gathered[...], axis=0)

    tile = early_step(16, z_n, early_z)
    early[1] = tile
    early_h[my_h] = tile
    offsets(high_n, lambda i: push(early.at[1], early_h.at[my_h], 15, "col", at_h(i)))

    arrive(4)
    total = jnp.sum(csums[...], axis=0)
    theta = from_row(total, 0) / from_row(total, 1)
    residual = hx - theta * x
    basis = jnp.concatenate([x, residual, p], axis=0)

    for k in (18, 17, 13, 14):
        arrive(k)
    loads[4].wait()

    def fetch(numbers, near_words, pair_words):
        guess, near_part, x_part, p_part = numbers
        near_code = near_words.astype(jnp.int32).astype(F32)
        pair_code = pair_words.astype(jnp.int32).astype(F32)
        x_wide = jnp.concatenate([pair_code[0:8], pair_code[8:16]], axis=1)
        p_wide = jnp.concatenate([pair_code[16:24], pair_code[24:32]], axis=1)
        near_wide = jnp.concatenate([near_code[0:8], near_code[8:16]], axis=1)
        res = near_part * near_wide + ((guess - theta) * x_part) * x_wide
        return res, jnp.concatenate([x_part * x_wide, res, p_part * p_wide], axis=0)

    forward, mirror, left, right = [], [], [], []
    for s in range(slots):
        live = jnp.where(s < count_ref[0], 1.0, 0.0).astype(F32)
        at_col, at_row = cols_ref[s], rows_ref[s]
        by_col, col_basis = fetch(
            col_numbers[s], cnear[lax.rem(at_col, near_n) * x_n + at_col // near_n], cpair[at_col])
        by_row, row_basis = fetch(
            row_numbers[s], rnear[at_row], rpair[lax.rem(at_row, z_n) * high_n + at_row // z_n])
        matrix = tiles[s]
        forward.append(split(dot(by_col.astype(BF16), matrix, NT) * live))
        mirror.append(split(dot(by_row.astype(BF16), matrix, NN) * live))
        left += [jnp.concatenate(forward[-1], axis=0), jnp.concatenate(mirror[-1], axis=0)]
        right += [jnp.concatenate(split(row_basis), axis=0), jnp.concatenate(split(col_basis), axis=0)]
    partial = dot(jnp.concatenate(left, axis=1), jnp.concatenate(right, axis=1), NT)

    g = partial[0:8] + partial[8:16]
    from_lane = iota((48, 256), 0)
    to_lane = lax.rem(iota((48, 256), 1), 32)
    spread = jnp.where((from_lane == to_lane) & (to_lane < 24) | (from_lane == to_lane + 24) & (to_lane < 24), 1.0, 0.0)
    g = dot(g, spread, NN, EXACT)
    g = jnp.sum(jnp.where(iota((8, 256), 1) // 32 == iota((8, 256), 0), g, 0.0), axis=0, keepdims=True)
    flat = jnp.concatenate([g[:, :128], g[:, 128:]], axis=0)
    late[...] = flat
    lrow[r] = flat
    each(rows_n, lambda i: push(late, lrow.at[r], 7, "row", along_row(i)))

    def spread_out(hot, parts, n, buffer):
        stack = jnp.concatenate([h for h, _ in parts] + [l for _, l in parts], axis=0)
        out = dot(hot, stack, NN)
        left, right = halves(out)
        out = jnp.concatenate([left.reshape(n, 8, 128), right.reshape(n, 8, 128)], axis=1)
        buffer[...] = out.astype(BF16)

    spread_out(row_hot, forward, cols_n, rsend)
    spread_out(col_hot, mirror, rows_n, csend)

    def push_parts(i):
        j, k = along_col(i), along_row(i)
        push(rsend.at[j], rrecv.at[c], 9, "col", j)
        push(csend.at[k], crecv.at[r], 10, "row", k)

    each(cols_n, push_parts)
    rrecv[c] = rsend[c]
    crecv[r] = csend[r]

    tile = early_step(15, high_n, early_h)
    shift = row_theta - theta
    in_rows = (lane >= 40) & (lane < 80)
    tile = tile + jnp.where(in_rows, shift * pltpu.roll(tile, 40, 1), 0.0)
    columns = jnp.where(lax.rem(lane, 40) == sub + 8, shift, 0.0)
    tile = tile + jnp.sum(columns, axis=0, keepdims=True) * pltpu.roll(tile, 8, 1)
    early[2] = tile
    early_x[my_x] = tile
    offsets(x_n, lambda i: push(early.at[2], early_x.at[my_x], 11, "row", at_x(i)))

    arrive(7)
    flat = jnp.sum(lrow[...], axis=0)
    lsum[...] = flat
    lcol[c] = flat
    each(cols_n, lambda i: push(lsum, lcol.at[c], 8, "col", along_col(i)))

    tile = early_step(11, x_n, early_x)
    early[3] = tile
    early_q[my_q] = tile
    offsets(near_n, lambda i: push(early.at[3], early_q.at[my_q], 12, "row", at_q(i)))

    coef = coef_ref[...]
    xn_ref[...] = dot(coef, basis, NN, EXACT)

    arrive(9)
    arrive(10)
    image = jnp.sum(rrecv[...].astype(F32), axis=0) + jnp.sum(crecv[...].astype(F32), axis=0)
    image = jnp.concatenate([image[0:8], image[8:16]], axis=1)
    hxn_ref[...] = dot(coef, jnp.concatenate([hx, image, hp], axis=0), NN, EXACT)

    scale = 1.0 / cells
    tile = early_step(12, near_n, early_q)
    products = jnp.concatenate([tile, pltpu.roll(tile, 88, 1), pltpu.roll(tile, 48, 1)], axis=0) * scale
    gs_ref[...] = products[:, :24]

    arrive(8)
    flat = jnp.sum(lcol[...], axis=0)
    flat = jnp.concatenate([flat[0:1], flat[1:2]], axis=1)
    mine = lax.rem(iota((24, 256), 1), 32) == iota((24, 256), 0)
    gather = jnp.where(iota((256, 128), 1) == 8 + iota((256, 128), 0) // 32, scale, 0.0)
    middle = dot(jnp.where(mine, flat, 0.0), gather, NN, EXACT)
    at = iota((24, 128), 1)
    full = jnp.where(at < 8, pltpu.roll(products, 104, 1), jnp.where(at < 16, middle, pltpu.roll(products, 112, 1)))
    gh_ref[...] = full[:, :24]

    for k, ref, n in table:
        wait(ref.at[pl.ds(0, n)], send.at[k])


def hand_over(xn_ref, hxn_ref, gh_ref, gs_ref, gh_out, gs_out, xn_out, hxn_out, sems):
    pairs = ((gh_ref, gh_out), (gs_ref, gs_out), (xn_ref, xn_out), (hxn_ref, hxn_out))
    copies = [pltpu.make_async_copy(a, b, sems.at[k]) for k, (a, b) in enumerate(pairs)]
    for copy in copies:
        copy.start()
    for copy in copies:
        copy.wait()


def finish(results):
    hbm = pl.BlockSpec(memory_space=pl.ANY)
    return pl.pallas_call(
        hand_over,
        out_shape=[jax.ShapeDtypeStruct(results[k].shape, F32) for k in (2, 3, 0, 1)],
        in_specs=[pl.BlockSpec(memory_space=pltpu.VMEM)] * 4,
        out_specs=[hbm] * 4,
        scratch_shapes=[pltpu.SemaphoreType.DMA((4,))],
        compiler_params=pltpu.CompilerParams(vmem_limit_bytes=LIMIT),
        name="hand_over",
    )(*results)


def body(x_block, hx_block, p_block, hp_block, tile_values, tile_rows, tile_cols, tile_count, coeffs):
    rows_n, cols_n = lax.axis_size("row"), lax.axis_size("col")
    states, length = x_block.shape
    slots = tile_values.shape[0]
    vmem = pl.BlockSpec(memory_space=pltpu.VMEM)
    word = jnp.int16
    hbm = pl.BlockSpec(memory_space=pl.ANY)
    outs = pl.pallas_call(
        functools.partial(kernel, rows_n, cols_n, length * rows_n * cols_n, slots),
        out_shape=(
            jax.ShapeDtypeStruct((states, length), F32),
            jax.ShapeDtypeStruct((states, length), F32),
            jax.ShapeDtypeStruct((24, 24), F32),
            jax.ShapeDtypeStruct((24, 24), F32),
        ),
        in_specs=[hbm] * 9,
        out_specs=(vmem,) * 4,
        scratch_shapes=[
            *[pltpu.VMEM((states, length), F32)] * 4,
            pltpu.VMEM(tile_values.shape, BF16),
            pltpu.SMEM((slots,), jnp.int32),
            pltpu.SMEM((slots,), jnp.int32),
            pltpu.SMEM((1,), jnp.int32),
            pltpu.VMEM((states, 24), F32),
            pltpu.VMEM((1, 128), F32),
            pltpu.VMEM((cols_n, 1, 128), F32),
            pltpu.VMEM((rows_n, 1, 128), F32),
            pltpu.VMEM((1, 128), F32),
            pltpu.VMEM((rows_n, 1, 128), F32),
            pltpu.VMEM((16, 128), word),
            pltpu.VMEM((cols_n, 16, 128), word),
            pltpu.VMEM((rows_n, 16, 128), word),
            pltpu.VMEM((32, 128), word),
            pltpu.VMEM((cols_n, 32, 128), word),
            pltpu.VMEM((rows_n, 32, 128), word),
            pltpu.VMEM((4, 8, 128), F32),
            pltpu.VMEM((rows_n // near_of(rows_n), 8, 128), F32),
            pltpu.VMEM((near_of(rows_n), 8, 128), F32),
            pltpu.VMEM((near_of(cols_n), 8, 128), F32),
            pltpu.VMEM((cols_n // near_of(cols_n), 8, 128), F32),
            pltpu.VMEM((2, 128), F32),
            pltpu.VMEM((rows_n, 2, 128), F32),
            pltpu.VMEM((2, 128), F32),
            pltpu.VMEM((cols_n, 2, 128), F32),
            pltpu.VMEM((cols_n, 16, 128), BF16),
            pltpu.VMEM((rows_n, 16, 128), BF16),
            pltpu.VMEM((cols_n, 16, 128), BF16),
            pltpu.VMEM((rows_n, 16, 128), BF16),
            pltpu.SemaphoreType.DMA((9,)),
            pltpu.SemaphoreType.DMA((19,)),
            pltpu.SemaphoreType.DMA((19,)),
        ],
        compiler_params=pltpu.CompilerParams(
            collective_id=0, has_side_effects=True, vmem_limit_bytes=LIMIT
        ),
        name="step",
    )(x_block, hx_block, p_block, hp_block, tile_values, tile_rows, tile_cols, tile_count, coeffs.T)
    return finish(outs)


def solution(mesh):
    both = ("row", "col")
    return jax.shard_map(
        body,
        mesh=mesh,
        in_specs=(
            P(None, both), P(None, both), P(None, both), P(None, both),
            P(both, None, None), P(both), P(both), P(both), P(),
        ),
        out_specs=(P(), P(), P(None, both), P(None, both)),
        check_vma=False,
    )
```

time: 67.1 us -> 56.9 us (0.85)
  local copies, waits for them, and re-layouts: 5.8 us -> 0 us
  Pallas kernels: 59.6 us -> 55.4 us
    unnamed x19 -> x0, local copies, waits for them, and re-layouts: 5.8 us -> none
    pallas_call x1, Pallas kernels: 59.6 us -> 54 us  [body(): pl.pallas_call(functools.partial(kernel, rows_n, cols_n, length * rows_n...]
    pallas_call x0 -> x1, Pallas kernels: none -> 1.4 us  [finish(): pl.pallas_call(hand_over, out_shape=[jax.ShapeDtypeStruct(results[k].shap...]
where the time goes in v2:
time: 56.9 us; the launch traced here: 56.7 us
  Pallas kernels  55.4 us (97%)
  between operations  1.29 us (2%)
    pallas_call x1, Pallas kernels, body(): pl.pallas_call(functools.partial(kernel, rows_n, cols_n, length * rows_n...  54 us
    pallas_call x1, Pallas kernels, finish(): pl.pallas_call(hand_over, out_shape=[jax.ShapeDtypeStruct(results[k].shap...  1.4 us

profile of v2, /device:TPU:1, one launch (start us, length us, event | category | flops | bytes accessed | tf_op | source)
XLA Modules:
  0.0 56.7 jit_solution(16325137485516094363)
XLA Ops:
  1.3 54.0 %step.1 = (f32[8,256]{1,0:T(8,128)}, f32[8,256]{1,0:T(8,128)}, f32[24,24]{1,0:T(8,128)}, f32[24,24]{1,0:T(8,128)}) custom-call(f32[8,256]{1,0:T(8,128)} %x_hbm.1, f32[8,256]{1,0:T(8,128)} %hx_hbm.1, f32[8,256]{1,0:T(8,128)} %p_hbm.1, f32[8,256]{1,0:T(8,128)} %hp_hbm.1, bf16[8,256,256]{2,1,0:T(8,128)(2,1)} %tiles_hbm.1, s32[8]{0:T(128)} %rows_hbm.1, ...), custom_call_target="tpu_custom_call" | custom-call | tf_op jit(solution)/shard_map/step/pallas_call | solution.py:377
  55.2 1.4 %hand_over.1 = (f32[24,24]{1,0:T(8,128)}, f32[24,24]{1,0:T(8,128)}, f32[8,256]{1,0:T(8,128)}, f32[8,256]{1,0:T(8,128)}) custom-call(f32[8,256]{1,0:T(8,128)} %get-tuple-element.8.xn_ref, f32[8,256]{1,0:T(8,128)} %get-tuple-element.9.hxn_ref, f32[24,24]{1,0:T(8,128)} %get-tuple-element.10.gh_ref, f32[24,24]{1,0:T(8,128)} %get-tuple-element.11.gs_ref), custom_call_target="tpu_custom_call" | custom-call | tf_op jit(solution)/shard_map/hand_over/pallas_call | solution.py:359

commit v3 on v2

--- a/solution.py
+++ b/solution.py
@@ -97,8 +97,24 @@
             device_id={axis: j}, device_id_type=MESH,
         ).start()
 
+    def offsets(n, f):
+        for i in range(1, n):
+            f(i)
+
+    def at_x(i):
+        return lax.rem(my_x + i, x_n) * near_n + my_q
+
+    def at_q(i):
+        return my_x * near_n + lax.rem(my_q + i, near_n)
+
+    def at_z(i):
+        return my_h * z_n + lax.rem(my_z + i, z_n)
+
+    def at_h(i):
+        return lax.rem(my_h + i, high_n) * z_n + my_z
+
     table = (
-        (0, rstat, cols_n - 1), (1, cstat, rows_n - 1), (4, csums, rows_n - 1),
+        (0, rstat, z_n - 1), (20, rstat, cols_n - z_n), (1, cstat, x_n - 1), (19, cstat, rows_n - x_n), (4, csums, rows_n - 1),
         (5, cpair, near_n - 1), (13, cpair, rows_n - near_n), (6, rpair, high_n - 1), (14, rpair, cols_n - high_n),
         (3, cnear, x_n - 1), (18, cnear, rows_n - x_n), (2, rnear, z_n - 1), (17, rnear, cols_n - z_n),
         (16, early_z, z_n - 1), (15, early_h, high_n - 1), (11, early_x, x_n - 1), (12, early_q, near_n - 1),
@@ -117,11 +133,11 @@
     ]
     for copy in loads:
         copy.start()
+    groups = ((z_n, "col", at_z), (high_n, "col", at_h), (x_n, "row", at_x), (near_n, "row", at_q))
     barrier = pltpu.get_barrier_semaphore()
-    each(cols_n, lambda i: pl.semaphore_signal(
-        barrier, inc=1, device_id={"col": along_col(i)}, device_id_type=MESH))
-    each(rows_n, lambda i: pl.semaphore_signal(
-        barrier, inc=1, device_id={"row": along_row(i)}, device_id_type=MESH))
+    for n, axis, at in groups:
+        offsets(n, lambda i: pl.semaphore_signal(
+            barrier, inc=1, device_id={axis: at(i)}, device_id_type=MESH))
     for k in (0, 1, 2, 3, 5, 6, 7, 8):
         loads[k].wait()
 
@@ -137,7 +153,7 @@
     row = to_row([cross, square, guess, near_step, x_step, p_step])
     stat[...] = row
     rstat[c] = row
-    cstat[r] = row
+    cstat[my_near] = row
     near_code = jnp.concatenate(halves(near_code), axis=0).astype(jnp.int32).astype(jnp.int16)
     near_send[...] = near_code
     rnear[c] = near_code
@@ -147,30 +163,14 @@
     rpair[my_slot] = pair
     cpair[r] = pair
 
-    pl.semaphore_wait(barrier, rows_n + cols_n - 2)
-
-    def offsets(n, f):
-        for i in range(1, n):
-            f(i)
-
-    def at_x(i):
-        return lax.rem(my_x + i, x_n) * near_n + my_q
-
-    def at_q(i):
-        return my_x * near_n + lax.rem(my_q + i, near_n)
-
-    def at_z(i):
-        return my_h * z_n + lax.rem(my_z + i, z_n)
-
-    def at_h(i):
-        return lax.rem(my_h + i, high_n) * z_n + my_z
-
-    each(cols_n, lambda i: push(stat, rstat.at[c], 0, "col", along_col(i)))
+    pl.semaphore_wait(barrier, sum(n - 1 for n, _, _ in groups))
+
+    offsets(z_n, lambda i: push(stat, rstat.at[c], 0, "col", at_z(i)))
     offsets(high_n, lambda i: push(pair_send, rpair.at[my_slot], 6, "col", at_h(i)))
     offsets(near_n, lambda i: push(pair_send, cpair.at[r], 5, "row", at_q(i)))
     offsets(z_n, lambda i: push(near_send, rnear.at[c], 2, "col", at_z(i)))
     offsets(x_n, lambda i: push(near_send, cnear.at[my_near], 3, "row", at_x(i)))
-    each(rows_n, lambda i: push(stat, cstat.at[r], 1, "row", along_row(i)))
+    offsets(x_n, lambda i: push(stat, cstat.at[my_near], 1, "row", at_x(i)))
 
     lane, sub = iota((8, 128), 1), iota((8, 128), 0)
     own_state = lax.rem(lane, 8) == sub
@@ -191,14 +191,18 @@
 
     arrive(5)
     onward(x_n, cpair, my_x * near_n, near_n, 13, "row", at_x)
-    arrive(3)
-    onward(near_n, cnear, my_q * x_n, x_n, 18, "row", at_q)
+    arrive(0)
+    onward(high_n, rstat, my_h * z_n, z_n, 20, "col", at_h)
     arrive(6)
     onward(z_n, rpair, my_z * high_n, high_n, 14, "col", at_z)
     arrive(2)
     onward(high_n, rnear, my_h * z_n, z_n, 17, "col", at_h)
-
-    arrive(0)
+    arrive(3)
+    onward(near_n, cnear, my_q * x_n, x_n, 18, "row", at_q)
+    arrive(1)
+    onward(near_n, cstat, my_q * x_n, x_n, 19, "row", at_q)
+
+    arrive(20)
     col_total = jnp.sum(rstat[...], axis=0)
     csum[...] = col_total
     csums[r] = col_total
@@ -214,12 +218,15 @@
     early_z[my_z] = tile
     offsets(z_n, lambda i: push(early.at[0], early_z.at[my_z], 16, "col", at_z(i)))
 
-    arrive(1)
+    arrive(19)
+
+    def near_slot(at):
+        return lax.rem(at, near_n) * x_n + at // near_n
 
     def numbers(row):
         return [from_row(row, place) for place in (2, 3, 4, 5)]
 
-    col_numbers = [numbers(cstat[cols_ref[s]]) for s in range(slots)]
+    col_numbers = [numbers(cstat[near_slot(cols_ref[s])]) for s in range(slots)]
     row_numbers = [numbers(rstat[rows_ref[s]]) for s in range(slots)]
 
     def early_step(k, n, gathered):
@@ -256,7 +263,7 @@
         live = jnp.where(s < count_ref[0], 1.0, 0.0).astype(F32)
         at_col, at_row = cols_ref[s], rows_ref[s]
         by_col, col_basis = fetch(
-            col_numbers[s], cnear[lax.rem(at_col, near_n) * x_n + at_col // near_n], cpair[at_col])
+            col_numbers[s], cnear[near_slot(at_col)], cpair[at_col])
         by_row, row_basis = fetch(
             row_numbers[s], rnear[at_row], rpair[lax.rem(at_row, z_n) * high_n + at_row // z_n])
         matrix = tiles[s]
@@ -362,7 +369,7 @@
         in_specs=[pl.BlockSpec(memory_space=pltpu.VMEM)] * 4,
         out_specs=[hbm] * 4,
         scratch_shapes=[pltpu.SemaphoreType.DMA((4,))],
-        compiler_params=pltpu.CompilerParams(vmem_limit_bytes=LIMIT),
+        compiler_params=pltpu.CompilerParams(vmem_limit_bytes=1 << 20),
         name="hand_over",
     )(*results)
 
@@ -377,10 +384,10 @@
     outs = pl.pallas_call(
         functools.partial(kernel, rows_n, cols_n, length * rows_n * cols_n, slots),
         out_shape=(
-            jax.ShapeDtypeStruct((states, length), F32),
-            jax.ShapeDtypeStruct((states, length), F32),
-            jax.ShapeDtypeStruct((24, 24), F32),
-            jax.ShapeDtypeStruct((24, 24), F32),
+            pltpu.VMEM((states, length), F32),
+            pltpu.VMEM((states, length), F32),
+            pltpu.VMEM((24, 24), F32),
+            pltpu.VMEM((24, 24), F32),
         ),
         in_specs=[hbm] * 9,
         out_specs=(vmem,) * 4,
@@ -416,8 +423,8 @@
             pltpu.VMEM((cols_n, 16, 128), BF16),
             pltpu.VMEM((rows_n, 16, 128), BF16),
             pltpu.SemaphoreType.DMA((9,)),
-            pltpu.SemaphoreType.DMA((19,)),
-            pltpu.SemaphoreType.DMA((19,)),
+            pltpu.SemaphoreType.DMA((21,)),
+            pltpu.SemaphoreType.DMA((21,)),
         ],
         compiler_params=pltpu.CompilerParams(
             collective_id=0, has_side_effects=True, vmem_limit_bytes=LIMIT

time: 56.9 us -> 54.1 us (0.951)
  Pallas kernels: 55.4 us -> 52.7 us
    pallas_call x1, Pallas kernels: 54 us -> 52 us  [body(): pl.pallas_call(functools.partial(kernel, rows_n, cols_n, length * rows_n...]
    pallas_call x1, Pallas kernels: 1.4 us -> 0.65 us  [finish(): pl.pallas_call(hand_over, out_shape=[jax.ShapeDtypeStruct(results[k].shap...]
where the time goes in v3:
time: 54.1 us; the launch traced here: 54 us
  Pallas kernels  52.7 us (97%)
  between operations  1.29 us (2%)
    pallas_call x1, Pallas kernels, body(): pl.pallas_call(functools.partial(kernel, rows_n, cols_n, length * rows_n...  52 us

profile of v3, /device:TPU:1, one launch (start us, length us, event | category | flops | bytes accessed | tf_op | source)
XLA Modules:
  0.0 54.0 jit_solution(5384192357922957736)
XLA Ops:
  1.3 52.0 %step.1 = (f32[8,256]{1,0:T(8,128)S(1)}, f32[8,256]{1,0:T(8,128)S(1)}, f32[24,24]{1,0:T(8,128)S(1)}, f32[24,24]{1,0:T(8,128)S(1)}) custom-call(f32[8,256]{1,0:T(8,128)} %x_hbm.1, f32[8,256]{1,0:T(8,128)} %hx_hbm.1, f32[8,256]{1,0:T(8,128)} %p_hbm.1, f32[8,256]{1,0:T(8,128)} %hp_hbm.1, bf16[8,256,256]{2,1,0:T(8,128)(2,1)} %tiles_hbm.1, s32[8]{0:T(128)} %rows_hbm.1, ...), custom_call_target="tpu_custom_call" | custom-call | tf_op jit(solution)/shard_map/step/pallas_call | solution.py:384
  53.3 0.6 %hand_over.1 = (f32[24,24]{1,0:T(8,128)}, f32[24,24]{1,0:T(8,128)}, f32[8,256]{1,0:T(8,128)}, f32[8,256]{1,0:T(8,128)}) custom-call(f32[8,256]{1,0:T(8,128)S(1)} %get-tuple-element.8.xn_ref, f32[8,256]{1,0:T(8,128)S(1)} %get-tuple-element.9.hxn_ref, f32[24,24]{1,0:T(8,128)S(1)} %get-tuple-element.10.gh_ref, f32[24,24]{1,0:T(8,128)S(1)} %get-tuple-element.11.gs_ref), custom_call_target="tpu_custom_call" | custom-call | tf_op jit(solution)/shard_map/hand_over/pallas_call | solution.py:366

commit v4 on v3

--- a/solution.py
+++ b/solution.py
@@ -98,7 +98,7 @@
         ).start()
 
     def offsets(n, f):
-        for i in range(1, n):
+        for i in sorted(range(1, n), key=lambda i: -min(i, n - i)):
             f(i)
 
     def at_x(i):
@@ -125,6 +125,11 @@
         ref, n = next((ref, n) for j, ref, n in table if j == k)
         wait(ref.at[pl.ds(0, n)], recv.at[k])
 
+    groups = ((z_n, "col", at_z), (high_n, "col", at_h), (x_n, "row", at_x), (near_n, "row", at_q))
+    barrier = pltpu.get_barrier_semaphore()
+    for n, axis, at in groups:
+        offsets(n, lambda i: pl.semaphore_signal(
+            barrier, inc=1, device_id={axis: at(i)}, device_id_type=MESH))
     loads = [
         pltpu.make_async_copy(a, b, load.at[k])
         for k, (a, b) in enumerate((
@@ -133,11 +138,6 @@
     ]
     for copy in loads:
         copy.start()
-    groups = ((z_n, "col", at_z), (high_n, "col", at_h), (x_n, "row", at_x), (near_n, "row", at_q))
-    barrier = pltpu.get_barrier_semaphore()
-    for n, axis, at in groups:
-        offsets(n, lambda i: pl.semaphore_signal(
-            barrier, inc=1, device_id={axis: at(i)}, device_id_type=MESH))
     for k in (0, 1, 2, 3, 5, 6, 7, 8):
         loads[k].wait()
 
@@ -327,26 +327,25 @@
     coef = coef_ref[...]
     xn_ref[...] = dot(coef, basis, NN, EXACT)
 
-    arrive(9)
-    arrive(10)
-    image = jnp.sum(rrecv[...].astype(F32), axis=0) + jnp.sum(crecv[...].astype(F32), axis=0)
-    image = jnp.concatenate([image[0:8], image[8:16]], axis=1)
-    hxn_ref[...] = dot(coef, jnp.concatenate([hx, image, hp], axis=0), NN, EXACT)
-
     scale = 1.0 / cells
     tile = early_step(12, near_n, early_q)
     products = jnp.concatenate([tile, pltpu.roll(tile, 88, 1), pltpu.roll(tile, 48, 1)], axis=0) * scale
     gs_ref[...] = products[:, :24]
-
-    arrive(8)
+    at = iota((24, 128), 1)
+    outer = jnp.where(at < 8, pltpu.roll(products, 104, 1), pltpu.roll(products, 112, 1))
+    known = dot(coef, jnp.concatenate([hx, jnp.zeros_like(hx), hp], axis=0), NN, EXACT)
+
+    for k in (9, 10, 8):
+        arrive(k)
+    image = jnp.sum(rrecv[...].astype(F32), axis=0) + jnp.sum(crecv[...].astype(F32), axis=0)
+    image = jnp.concatenate([image[0:8], image[8:16]], axis=1)
+    hxn_ref[...] = known + dot(coef[:, 8:16], image, NN, EXACT)
     flat = jnp.sum(lcol[...], axis=0)
     flat = jnp.concatenate([flat[0:1], flat[1:2]], axis=1)
     mine = lax.rem(iota((24, 256), 1), 32) == iota((24, 256), 0)
     gather = jnp.where(iota((256, 128), 1) == 8 + iota((256, 128), 0) // 32, scale, 0.0)
     middle = dot(jnp.where(mine, flat, 0.0), gather, NN, EXACT)
-    at = iota((24, 128), 1)
-    full = jnp.where(at < 8, pltpu.roll(products, 104, 1), jnp.where(at < 16, middle, pltpu.roll(products, 112, 1)))
-    gh_ref[...] = full[:, :24]
+    gh_ref[...] = jnp.where((at >= 8) & (at < 16), middle, outer)[:, :24]
 
     for k, ref, n in table:
         wait(ref.at[pl.ds(0, n)], send.at[k])

time: 54.1 us -> 54.1 us (level)
  no operation moved by 1% of the time
where the time goes in v4:
time: 54.1 us; the launch traced here: 53.9 us
  Pallas kernels  52.6 us (97%)
  between operations  1.29 us (2%)
    pallas_call x1, Pallas kernels, body(): pl.pallas_call(functools.partial(kernel, rows_n, cols_n, length * rows_n...  52 us

profile of v4, /device:TPU:1, one launch (start us, length us, event | category | flops | bytes accessed | tf_op | source)
XLA Modules:
  0.0 53.9 jit_solution(16192899341987310935)
XLA Ops:
  1.3 52.0 %step.1 = (f32[8,256]{1,0:T(8,128)S(1)}, f32[8,256]{1,0:T(8,128)S(1)}, f32[24,24]{1,0:T(8,128)S(1)}, f32[24,24]{1,0:T(8,128)S(1)}) custom-call(f32[8,256]{1,0:T(8,128)} %x_hbm.1, f32[8,256]{1,0:T(8,128)} %hx_hbm.1, f32[8,256]{1,0:T(8,128)} %p_hbm.1, f32[8,256]{1,0:T(8,128)} %hp_hbm.1, bf16[8,256,256]{2,1,0:T(8,128)(2,1)} %tiles_hbm.1, s32[8]{0:T(128)} %rows_hbm.1, ...), custom_call_target="tpu_custom_call" | custom-call | tf_op jit(solution)/shard_map/step/pallas_call | solution.py:383
  53.2 0.6 %hand_over.1 = (f32[24,24]{1,0:T(8,128)}, f32[24,24]{1,0:T(8,128)}, f32[8,256]{1,0:T(8,128)}, f32[8,256]{1,0:T(8,128)}) custom-call(f32[8,256]{1,0:T(8,128)S(1)} %get-tuple-element.8.xn_ref, f32[8,256]{1,0:T(8,128)S(1)} %get-tuple-element.9.hxn_ref, f32[24,24]{1,0:T(8,128)S(1)} %get-tuple-element.10.gh_ref, f32[24,24]{1,0:T(8,128)S(1)} %get-tuple-element.11.gs_ref), custom_call_target="tpu_custom_call" | custom-call | tf_op jit(solution)/shard_map/hand_over/pallas_call | solution.py:365
